TPU v7x, 768 devices: a whole 4x8x12 slice. The times are simulated.
768 devices in a mesh: frame: 24 (over z, x_lo), pipe: 4 (over x_hi, core), dp: 8 (over y).
Axes of the slice: x: 4 (x_hi: 2, x_lo: 2; x = x_hi * 2 + x_lo), y: 8, z: 12, core: 2. Of those that a mesh axis runs over, the one named last changes fastest.
Arguments:
- acts: bfloat16 [4, 8, 192, 24, 1280], P('pipe', 'dp', 'frame'), may hold values from -18 to 18
- cotangent: bfloat16 [4, 8, 192, 24, 1280], P('pipe', 'dp', 'frame'), may hold values from -6 to 6
- w_query: bfloat16 [4, 1280, 768], P('pipe'), may hold values from -0.15625 to 0.15625
- w_key: bfloat16 [4, 1280, 768], P('pipe'), may hold values from -0.15625 to 0.15625
- w_value: bfloat16 [4, 1280, 768], P('pipe'), may hold values from -0.15625 to 0.15625
- w_out: bfloat16 [4, 1280, 768], P('pipe'), may hold values from -0.21875 to 0.21875
Outputs:
- sent_grad: bfloat16 [4, 8, 192, 24, 1280], P('pipe', 'dp', 'frame')
- grad_value: float32 [4, 1280, 768], P('pipe', None, ('frame', 'dp'))
All inputs are finite; a program needn't handle non-finite values.
Results may differ from a plain program's by a relative error of at most 0.017.
The roundings to bfloat16 on the way count: a program that leaves them out, or rounds other values in their place, can miss the bound.
Values may be sent and summed in bfloat16 or wider, within the bound.
A program may use at most 64 MiB of HBM per device.

v0:
```python
import jax
import jax.numpy as jnp
from jax import lax
from jax.sharding import Mesh
from jax.sharding import PartitionSpec as P

HEADS = 12
HEAD_DIM = 64
FRAME = ("frame_0", "frame_1")
FRAME_DP = ("frame_0", "frame_1", "dp")


score_scale = 0.125


def in_one_piece(arrays, axis, split_dim, concat_dim, along):
    both = jnp.concatenate(arrays, axis=along)
    filled, at, outs = (
        lax.all_to_all(both, axis, split_axis=split_dim, concat_axis=concat_dim, tiled=True),
        0,
        [],
    )
    for a in arrays:
        outs.append(lax.slice_in_dim(filled, at, at + a.shape[along], axis=along))
        at += a.shape[along]
    return tuple(outs)


def shifted(shard, axis, by):
    count = lax.axis_size(axis)
    pairs = [(i, i + by) for i in range(count) if 0 <= i + by < count]
    return lax.ppermute(shard, axis, pairs)


def sum_by_axis(shard, axes, dim):
    if not axes:
        return shard
    nearer = lax.psum_scatter(shard, axes[0], scatter_dimension=dim, tiled=True)
    return sum_by_axis(nearer, axes[1:], dim)


def in_blocks(shard, dim, count):
    before, after = (shard.shape[:dim], shard.shape[dim + 1 :])
    return jnp.moveaxis(shard.reshape(*before, count, -1, *after), dim, 0)


def sum_at_owner(shard, axis, dim):
    count = lax.axis_size(axis)
    parts = lax.all_to_all(in_blocks(shard, dim, count), axis, 0, 0, tiled=True)
    return jnp.sum(parts.astype(jnp.float32), axis=0)


def attend_back(inputs, projected, w_query, w_key, w_value):
    frames = inputs.shape[0]
    places = inputs.shape[1]

    def project_heads(weight):
        result = jnp.dot(inputs, weight, preferred_element_type=jnp.float32).astype(jnp.bfloat16)
        return result.reshape(frames, places, HEADS, HEAD_DIM)

    queries = project_heads(w_query)
    key_rows = project_heads(w_key)
    values = project_heads(w_value)
    scores = (
        jnp.einsum("iphd,jphd->phij", queries, key_rows, preferred_element_type=jnp.float32)
        * score_scale
    )
    probability = jax.nn.softmax(scores, axis=-1)
    prob_short = probability.astype(jnp.bfloat16)
    proj_heads = projected.reshape(frames, places, HEADS, HEAD_DIM)
    grad_prob = jnp.einsum(
        "iphd,jphd->phij", proj_heads, values, preferred_element_type=jnp.float32
    )
    value_grad = jnp.einsum(
        "phij,iphd->jphd", prob_short, proj_heads, preferred_element_type=jnp.float32
    ).astype(jnp.bfloat16)
    score_grad = probability * (
        grad_prob - jnp.sum(grad_prob * probability, axis=-1, keepdims=True)
    )
    score_short = score_grad.astype(jnp.bfloat16)
    query_grad = (
        jnp.einsum("phij,jphd->iphd", score_short, key_rows, preferred_element_type=jnp.float32)
        * score_scale
    ).astype(jnp.bfloat16)
    key_grad = (
        jnp.einsum("phij,iphd->jphd", score_short, queries, preferred_element_type=jnp.float32)
        * score_scale
    ).astype(jnp.bfloat16)
    inner = HEADS * HEAD_DIM
    query_grad = query_grad.reshape(frames, places, inner)
    key_grad = key_grad.reshape(frames, places, inner)
    value_grad = value_grad.reshape(frames, places, inner)
    branch = jnp.einsum("fpj,cj->fpc", query_grad, w_query, preferred_element_type=jnp.float32)
    branch = branch + jnp.einsum("fpj,cj->fpc", key_grad, w_key, preferred_element_type=jnp.float32)
    branch = branch + jnp.einsum(
        "fpj,cj->fpc", value_grad, w_value, preferred_element_type=jnp.float32
    )
    branch = branch.astype(jnp.bfloat16)
    weight_grad = jnp.einsum("fpc,fpj->cj", inputs, value_grad, preferred_element_type=jnp.float32)
    return (branch, weight_grad)


def body(acts, cotangent, w_query, w_key, w_value, w_out):
    inputs = acts[0, 0]
    upstream = cotangent[0, 0]
    query_weight = w_query[0]
    key_weight = w_key[0]
    value_weight = w_value[0]
    out_weight = w_out[0]
    projected = jnp.dot(upstream, out_weight, preferred_element_type=jnp.float32).astype(
        jnp.bfloat16
    )
    row_inputs, row_projected = in_one_piece((inputs, projected), FRAME, 1, 0, 2)
    branch, value_grad = attend_back(
        row_inputs, row_projected, query_weight, key_weight, value_weight
    )
    frame_branch = lax.all_to_all(branch, FRAME, split_axis=0, concat_axis=1, tiled=True)
    frame_result = (upstream.astype(jnp.float32) + frame_branch.astype(jnp.float32)).astype(
        jnp.bfloat16
    )
    sent_grad = shifted(frame_result[None, None], "pipe", -1)
    value_middle = sum_by_axis(value_grad.astype(jnp.bfloat16), FRAME, 1).astype(jnp.float32)
    value_part = sum_at_owner(value_middle.astype(jnp.bfloat16), "dp", 1)
    return (sent_grad, value_part[None])


def solution(mesh):
    finer = Mesh(
        mesh.devices.reshape(12, 2, mesh.shape["pipe"], mesh.shape["dp"]),
        ("frame_0", "frame_1", "pipe", "dp"),
    )
    placed = (
        P("pipe", "dp", FRAME, None, None),
        P("pipe", "dp", FRAME, None, None),
        P("pipe", None, None),
        P("pipe", None, None),
        P("pipe", None, None),
        P("pipe", None, None),
    )
    return jax.shard_map(
        body,
        mesh=finer,
        in_specs=placed,
        out_specs=(P("pipe", "dp", FRAME, None, None), P("pipe", None, FRAME_DP)),
        check_vma=False,
    )
```

profile of v0, /device:TPU:6, one launch (start us, length us, event | category | flops | bytes accessed | tf_op | source)
XLA Modules:
  0.0 191.1 jit_solution(5861892351076020810)
XLA Ops:
  7.2 2.4 %fusion.20 = bf16[8,24,768]{2,1,0:T(8,128)(2,1)S(1)} fusion(bf16[1,1280,768]{2,1,0:T(8,128)(2,1)} %param.11, bf16[1,1,8,24,1280]{4,3,2,1,0:T(8,128)(2,1)} %param.7), kind=kOutput, calls=%fused_computation.28 | convolution fusion | flops 377634816 | bytes 2752512 | tf_op jit(solution)/shard_map/dot_general | solution.py:110
  9.9 48.1 %all_to_all.32 = bf16[8,24,2048]{2,0,1:T(8,128)(2,1)S(1)} all-to-all(bf16[8,24,2048]{2,0,1:T(8,128)(2,1)S(1)} %pad_maximum_fusion), channel_id=1, replica_groups=mesh['frame_0'=12,'frame_1'=2,'pipe'=4,'dp'=8] {'frame_0','frame_1'}, dimensions={1} | all-to-all | bytes 1572864 | tf_op jit(solution)/shard_map/all_to_all | solution.py:19
  58.1 1.3 fusion.26
  59.4 1.1 copy.30
  60.5 3.0 %fusion.29 = bf16[192,768]{1,0:T(8,128)(2,1)} fusion(bf16[1,1280,768]{2,1,0:T(8,128)(2,1)} %param.10, bf16[192,1,2048]{2,0,1:T(8,128)(2,1)S(1)} %bitcast.95), kind=kOutput, calls=%fused_computation.31 | convolution fusion | flops 377634816 | bytes 2752512 | tf_op jit(solution)/shard_map/dot_general | solution.py:58
  63.5 1.9 copy.32
  65.4 0.9 copy.31
  66.3 2.8 %fusion.23 = bf16[192,768]{1,0:T(8,128)(2,1)} fusion(bf16[1,1280,768]{2,1,0:T(8,128)(2,1)} %param.9, bf16[192,1,2048]{2,0,1:T(8,128)(2,1)S(1)} %bitcast.96), kind=kOutput, calls=%fused_computation.29 | convolution fusion | flops 377634816 | bytes 2752512 | tf_op jit(solution)/shard_map/dot_general | solution.py:58
  69.1 1.1 copy.29
  70.3 2.4 %fusion.39 = (f32[12,192]{1,0:T(8,128)S(1)}, f32[12,192,192]{1,2,0:T(8,128)}) fusion(bf16[192,12,64]{0,2,1:T(8,128)(2,1)S(1)} %bitcast.103, bf16[192,12,64]{0,2,1:T(8,128)(2,1)S(1)} %bitcast.105), kind=kOutput, calls=%fused_computation.44 | convolution fusion | flops 57950400 | bytes 2368512 | tf_op jit(solution)/shard_map/sub | solution.py:68
  72.7 2.3 %convolution_convert_fusion.1 = bf16[12,64,192]{2,1,0:T(8,128)(2,1)S(1)} fusion(bf16[192,12,64]{0,2,1:T(8,128)(2,1)} %bitcast.108, f32[12,192,192]{1,2,0:T(8,128)} %get-tuple-element.3, f32[12,192]{1,0:T(8,128)S(1)} %get-tuple-element.2), kind=kOutput, calls=%fused_computation.27 | convolution fusion | flops 57655296 | bytes 2368512 | tf_op jit(solution)/shard_map/phij,iphd->jphd/dot_general | solution.py:74
  75.0 2.0 %convolution_convert_fusion = bf16[1280,768]{0,1:T(8,128)(2,1)} fusion(bf16[192,768]{0,1:T(8,128)(2,1)S(1)} %bitcast.99, bf16[192,1,2048]{2,0,1:T(8,128)(2,1)S(1)} %bitcast.97), kind=kOutput, calls=%fused_computation.1 | convolution fusion | flops 378470400 | bytes 2850816 | tf_op jit(solution)/shard_map/fpc,fpj->cj/dot_general | solution.py:99
  77.0 0.9 copy-done.10
  78.1 2.4 %multiply_reduce_fusion = (f32[12,192]{1,0:T(8,128)S(1)}, f32[12,192,192]{1,2,0:T(8,128)S(1)}) fusion(f32[12,192,192]{1,2,0:T(8,128)} %get-tuple-element.3, f32[12,192]{1,0:T(8,128)S(1)} %get-tuple-element.2, bf16[192,12,64]{0,2,1:T(8,128)(2,1)S(1)} %bitcast.109, bf16[192,12,64]{0,2,1:T(8,128)(2,1)S(1)} %bitcast.107), kind=kOutput, calls=%fused_computation.7 | convolution fusion | flops 57947904 | bytes 4147200 | tf_op jit(solution)/shard_map/iphd,jphd->phij/dot_general | solution.py:71
  85.9 0.8 fusion.2
  87.2 1.0 reduce.6
  88.4 32.1 %all_to_all.33 = bf16[24,2,5120]{2,1,0:T(2,128)(2,1)S(1)} all-to-all(bf16[24,2,5120]{2,1,0:T(2,128)(2,1)S(1)} %reshape.139), channel_id=1, replica_groups=mesh['frame_0'=12,'frame_1'=2,'pipe'=4,'dp'=8] {'frame_0','frame_1'}, dimensions={0} | all-to-all | bytes 983040 | tf_op jit(solution)/shard_map/all_to_all | solution.py:117
  120.9 1.0 convert.3
  122.3 1.9 %collective-permute-start = (bf16[1,1,8,24,1280]{4,3,2,1,0:T(8,128)(2,1)S(1)}, bf16[1,1,8,24,1280]{4,3,2,1,0:T(8,128)(2,1)S(1)}, u32[]{:S(2)}, u32[]{:S(2)}) collective-permute-start(bf16[1,1,8,24,1280]{4,3,2,1,0:T(8,128)(2,1)S(1)} %fusion.34), channel_id=1, source_target_pairs={{8,0},{16,8},{24,16},{9,1},{17,9},{25,17},{10,2},{18,10},{26,18},{... | collective-permute-start | bytes 1474568 | tf_op jit(solution)/shard_map/ppermute | solution.py:32
  124.2 19.6 %reduce-scatter.3.cloned.1.call-done = bf16[1280,64]{0,1:T(8,128)(2,1)} async-done(((bf16[1280,768]{0,1:T(8,128)(2,1)}), bf16[1280,64]{0,1:T(8,128)(2,1)}) %reduce-scatter.3.cloned.1.call-update) | async-done | bytes 163856 | tf_op jit(solution)/shard_map/reduce_scatter | solution.py:38
  143.9 22.2 %reduce-scatter.5.cloned.1.call-done = bf16[1280,32]{0,1:T(8,128)(2,1)} async-done(((bf16[1280,64]{0,1:T(8,128)(2,1)}), bf16[1280,32]{0,1:T(8,128)(2,1)}) %reduce-scatter.5.cloned.1.call-update) | async-done | bytes 81936 | tf_op jit(solution)/shard_map/reduce_scatter | solution.py:38
  166.0 1.5 reshape.135
  167.6 6.7 %all-to-all-start.2 = ((bf16[8,1280,4]{1,2,0:T(4,128)(2,1)}), bf16[8,1280,4]{1,2,0:T(4,128)(2,1)S(1)}, u32[]{:S(2)}, u32[]{:S(2)}) async-start(bf16[8,1280,4]{1,2,0:T(4,128)(2,1)} %bitcast.32), calls=%async_computation.4 | async-start | bytes 163840 | tf_op jit(solution)/shard_map/all_to_all | solution.py:49
  174.3 8.5 %all-to-all-done.2 = bf16[8,1280,4]{1,2,0:T(4,128)(2,1)S(1)} async-done(((bf16[8,1280,4]{1,2,0:T(4,128)(2,1)}), bf16[8,1280,4]{1,2,0:T(4,128)(2,1)S(1)}, u32[]{:S(2)}, u32[]{:S(2)}) %all-to-all-start.2) | async-done | bytes 81952 | tf_op jit(solution)/shard_map/all_to_all | solution.py:49
  (43 shorter events, 8.7 us)
Async XLA Ops:
  7.2 50.9 %copy-start = (bf16[1,1280,768]{2,1,0:T(8,128)(2,1)S(1)}, bf16[1,1280,768]{2,1,0:T(8,128)(2,1)}, u32[]{:S(2)}) copy-start(bf16[1,1280,768]{2,1,0:T(8,128)(2,1)} %param.8) | copy-start | bytes 5898244
  7.2 2.6 %copy-start.9 = (bf16[1,1,8,24,1280]{4,3,2,1,0:T(8,128)(2,1)S(1)}, bf16[1,1,8,24,1280]{4,3,2,1,0:T(8,128)(2,1)}, u32[]{:S(2)}) copy-start(bf16[1,1,8,24,1280]{4,3,2,1,0:T(8,128)(2,1)} %param.6) | copy-start | bytes 1474564
  7.2 136.6 %reduce-scatter.3.cloned.1.call-start = ((), (), s32[]{:S(2)}) async-start(), calls=%async_computation.5 | async-start | bytes 2129920 | tf_op jit(solution)/shard_map/reduce_scatter | solution.py:38
  60.5 9.7 %copy-start.5 = (bf16[192,768]{0,1:T(8,128)(2,1)}, bf16[192,768]{0,1:T(8,128)(2,1)S(1)}, u32[]{:S(2)}) copy-start(bf16[192,768]{0,1:T(8,128)(2,1)S(1)} %copy.30) | copy-start | bytes 884740
  70.2 2.4 %copy-start.7 = (bf16[192,768]{0,1:T(8,128)(2,1)}, bf16[192,768]{0,1:T(8,128)(2,1)S(1)}, u32[]{:S(2)}) copy-start(bf16[192,768]{0,1:T(8,128)(2,1)S(1)} %copy.29) | copy-start | bytes 884740
  76.9 1.0 copy-start.10
  76.9 1.1 copy-start.11
  77.0 89.1 %reduce-scatter.5.cloned.1.call-start = ((), (), s32[]{:S(2)}) async-start(), calls=%async_computation.6 | async-start | bytes 245760 | tf_op jit(solution)/shard_map/reduce_scatter | solution.py:38
  78.1 2.4 %copy-start.1 = (f32[12,192,192]{1,2,0:T(8,128)S(1)}, f32[12,192,192]{1,2,0:T(8,128)}, u32[]{:S(2)}) copy-start(f32[12,192,192]{1,2,0:T(8,128)} %get-tuple-element.3) | copy-start | bytes 5308420
  80.4 1.0 copy-start.6
  81.4 1.0 copy-start.8
  82.8 1.5 copy-start.2
  84.3 1.5 copy-start.3
  120.9 1.0 copy-start.4
  122.3 52.1 %collective-permute-start = (bf16[1,1,8,24,1280]{4,3,2,1,0:T(8,128)(2,1)S(1)}, bf16[1,1,8,24,1280]{4,3,2,1,0:T(8,128)(2,1)S(1)}, u32[]{:S(2)}, u32[]{:S(2)}) collective-permute-start(bf16[1,1,8,24,1280]{4,3,2,1,0:T(8,128)(2,1)S(1)} %fusion.34), channel_id=1, source_target_pairs={{8,0},{16,8},{24,16},{9,1},{17,9},{25,17},{10,2},{18,10},{26,18},{... | collective-permute-start | bytes 1474568 | tf_op jit(solution)/shard_map/ppermute | solution.py:32
  167.6 15.3 %all-to-all-start.2 = ((bf16[8,1280,4]{1,2,0:T(4,128)(2,1)}), bf16[8,1280,4]{1,2,0:T(4,128)(2,1)S(1)}, u32[]{:S(2)}, u32[]{:S(2)}) async-start(bf16[8,1280,4]{1,2,0:T(4,128)(2,1)} %bitcast.32), calls=%async_computation.4 | async-start | bytes 163840 | tf_op jit(solution)/shard_map/all_to_all | solution.py:49
Sparse Core Ops, SparseCore 0:
  77.1 66.6 reduce-scatter.2
  146.9 19.1 reduce-scatter.4
where the time goes:
time: 192 us; the launch traced here: 191 us
  blocking collectives  80.2 us (42%)
  waiting for transfers between devices  50.4 us (26%)
  matrix products  21.8 us (11%)
  between operations  14.3 us (7%)
  local copies, waits for them, and re-layouts  12.2 us (6%)
  starting transfers between devices  8.73 us (5%)
  other arithmetic  3.48 us (2%)
    all_to_all x1, blocking collectives, in_one_piece(): lax.all_to_all(both, axis, split_axis=split_dim, concat_axis=concat_dim,...  48.1 us
    reduce_scatter x2, waiting for transfers between devices, sum_by_axis(): nearer = lax.psum_scatter(shard, axes[0], scatter_dimension=dim, tiled=True)  41.8 us
    all_to_all x1, blocking collectives, body(): lax.all_to_all(branch, FRAME, split_axis=0, concat_axis=1, tiled=True)  32.1 us
    all_to_all x1, waiting for transfers between devices, sum_at_owner(): parts = lax.all_to_all(in_blocks(shard, dim, count), axis, 0, 0, tiled=True)  8.55 us
    dot_general x3, matrix products, project_heads(): jnp.dot(inputs, weight, preferred_element_type=jnp.float32)  7.05 us
    all_to_all x1, starting transfers between devices, sum_at_owner(): parts = lax.all_to_all(in_blocks(shard, dim, count), axis, 0, 0, tiled=True)  6.73 us
    unnamed x28, local copies, waits for them, and re-layouts  5.03 us
    convert_element_type x3, local copies, waits for them, and re-layouts, project_heads(): jnp.dot(inputs, weight, preferred_element_type=jnp.float32)  4.15 us
  transfers between devices with their start and end apart: 4, of which 3 were waited for; matrix products, arithmetic and copies ran while one was open for 6% of the time, Pallas kernels for 0%

commit v1 on v0

v1 whole, which is shorter than its diff:
```python
import functools

import jax
import jax.numpy as jnp
from jax import lax
from jax.experimental import pallas as pl
from jax.experimental.pallas import tpu as pltpu
from jax.sharding import PartitionSpec as P

HEADS = 12
HEAD_DIM = 64
PAIR = 2 * HEAD_DIM
PAIRS = HEADS // 2
SCALE = 0.125

BF16 = jnp.bfloat16
F32 = jnp.float32
MESH = pl.DeviceIdType.MESH

NN = (((1,), (0,)), ((), ()))
NT = (((1,), (1,)), ((), ()))
TN = (((0,), (0,)), ((), ()))


def dot(a, b, dims=NN):
    return lax.dot_general(a, b, dims, preferred_element_type=F32)


def wait_bytes(ref, sem):
    pltpu.make_async_copy(ref, ref, sem).wait()


def kernel(
    nf,
    ny,
    np_,
    acts,
    cot,
    w_query,
    w_key,
    w_value,
    w_out,
    sent,
    gvalue,
    acts_rx,
    proj_rx,
    proj_tx,
    cot_v,
    cot_rx,
    ret_tx,
    ret_rx,
    wq_v,
    wk_v,
    wv_v,
    wo_v,
    q_s,
    k_s,
    v_s,
    vg_s,
    dq_s,
    dk_s,
    order,
    vgt_b,
    prob,
    gv,
    rs_tx,
    rs_rx,
    fin_f,
    fin_tx,
    fin_rx,
    local_sem,
    acts_sem,
    proj_sem,
    cot_sem,
    ret_sem,
    fin_sem,
    rs_send,
    rs_recv,
):
    me = lax.axis_index("frame")
    pipe = lax.axis_index("pipe")
    clip = lax.axis_index("dp")
    per = acts_rx.shape[1]
    chans = acts_rx.shape[2]
    inner = proj_rx.shape[2]
    rows = nf * per
    half = chans // 2
    reach = ny // 2
    messages = 2 * reach - 1
    mine = gvalue.shape[0]
    size = mine * nf

    loads = []
    for i, (src, dst) in enumerate(
        (
            (w_out, wo_v),
            (cot, cot_v),
            (acts.at[me], acts_rx.at[0]),
            (w_query, wq_v),
            (w_key, wk_v),
            (w_value, wv_v),
        )
    ):
        load = pltpu.make_async_copy(src, dst, local_sem.at[i])
        load.start()
        loads.append(load)

    barrier = pltpu.get_barrier_semaphore()
    up = lax.rem(clip + 1, ny)
    down = lax.rem(clip + ny - 1, ny)

    def greet(k, carry):
        pl.semaphore_signal(
            barrier, inc=1, device_id={"frame": lax.rem(me + k, nf)}, device_id_type=MESH
        )
        return carry

    lax.fori_loop(1, nf, greet, 0)
    for y in (up, down):
        pl.semaphore_signal(barrier, inc=1, device_id={"dp": y}, device_id_type=MESH)
    pl.semaphore_signal(
        barrier, inc=1, device_id={"pipe": lax.rem(pipe + 1, np_)}, device_id_type=MESH
    )
    pl.semaphore_wait(barrier, nf + 2)

    def shift_of(i):
        near = lax.div(i, 2)
        odd = lax.rem(i, 2)
        return (near + 1) * (1 - odd) + (nf - 1 - near) * odd

    def spread(src_of, rx, sems):
        def one(i, carry):
            k = shift_of(i)
            to = lax.rem(me + k, nf)
            pltpu.make_async_remote_copy(
                src_ref=src_of(to),
                dst_ref=rx.at[k],
                send_sem=sems.at[0],
                recv_sem=sems.at[1],
                device_id={"frame": to},
                device_id_type=MESH,
            ).start()
            return carry

        lax.fori_loop(0, nf - 1, one, 0)

    others = pl.ds(1, nf - 1)

    spread(lambda to: acts.at[to], acts_rx, acts_sem)

    loads[0].wait()
    loads[1].wait()
    projected = dot(cot_v[...].reshape(rows, chans), wo_v[...]).astype(BF16)
    proj_tx[...] = projected.reshape(nf, per, inner)
    proj_rx[0] = proj_tx[me]
    spread(lambda to: proj_tx.at[to], proj_rx, proj_sem)

    @pl.when(pipe > 0)
    def _():
        pltpu.make_async_remote_copy(
            src_ref=cot,
            dst_ref=cot_rx,
            send_sem=cot_sem.at[0],
            recv_sem=cot_sem.at[1],
            device_id={"pipe": pipe - 1},
            device_id_type=MESH,
        ).start()

    at = lax.broadcasted_iota(jnp.int32, (inner, inner), 0)
    column = lax.rem(lax.div(at, mine), nf) * (ny * mine) + lax.div(at, size) * mine + lax.rem(at, mine)
    order[...] = jnp.where(
        column == lax.broadcasted_iota(jnp.int32, (inner, inner), 1), 1.0, 0.0
    ).astype(BF16)

    for load in loads[2:]:
        load.wait()
    wait_bytes(acts_rx.at[others], acts_sem.at[1])
    inputs = acts_rx[...].reshape(rows, chans)
    q_s[...] = dot(inputs, wq_v[...]).astype(BF16)
    k_s[...] = dot(inputs, wk_v[...]).astype(BF16)
    v_s[...] = dot(inputs, wv_v[...]).astype(BF16)
    wait_bytes(proj_rx.at[others], proj_sem.at[1])
    lane = lax.broadcasted_iota(jnp.int32, (1, PAIR), 1)
    masks = [jnp.where(lane // HEAD_DIM == e, 1.0, 0.0).astype(BF16) for e in range(2)]

    for pair in range(PAIRS):
        cols = pl.ds(pair * PAIR, PAIR)
        q = q_s[:, cols]
        k = k_s[:, cols]
        p = proj_rx[:, :, cols].reshape(rows, PAIR)
        total = jnp.zeros((rows, PAIR), F32)
        for e in range(2):
            scores = dot(k * masks[e], q, NT) * SCALE
            scores = jnp.exp(scores - jnp.max(scores, axis=0, keepdims=True))
            scores = scores * (1.0 / jnp.sum(scores, axis=0, keepdims=True))
            prob[2 * pair + e] = scores
            total = total + dot(scores.astype(BF16), p * masks[e])
        vg_s[:, cols] = total.astype(BF16)

    vgt_b[...] = dot(order[...], vg_s[...], NT).astype(BF16)
    for y in range(ny):
        gv[y] = dot(vgt_b[y * size : (y + 1) * size, :], inputs)

    def own(o, h):
        return gv[o, :, h * half : (h + 1) * half]

    def ring(d, j):
        return pltpu.make_async_remote_copy(
            src_ref=rs_tx.at[d, j],
            dst_ref=rs_rx.at[d, j],
            send_sem=rs_send.at[d, j],
            recv_sem=rs_recv.at[d, j],
            device_id={"dp": (up, down)[d]},
            device_id_type=MESH,
        )

    def ring_step(j):
        away = reach - (j + 1) // 2
        for d in range(2):
            h = (j + d) % 2
            o = lax.rem(clip + (away if d == 0 else ny - away), ny)
            value = own(o, h)
            if j >= 2:
                ring(d, j - 2).wait_recv()
                value = value + rs_rx[d, j - 2].astype(F32)
            rs_tx[d, j] = value.astype(BF16)
            ring(d, j).start()

    for j in range(min(2, messages)):
        ring_step(j)

    for pair in range(PAIRS):
        cols = pl.ds(pair * PAIR, PAIR)
        q = q_s[:, cols]
        k = k_s[:, cols]
        v = v_s[:, cols]
        p = proj_rx[:, :, cols].reshape(rows, PAIR)
        dq = jnp.zeros((rows, PAIR), F32)
        dk = jnp.zeros((rows, PAIR), F32)
        for e in range(2):
            probability = prob[2 * pair + e]
            grad = dot(v * masks[e], p, NT)
            mean = jnp.sum(grad * probability, axis=0, keepdims=True)
            grad = (probability * (grad - mean)).astype(BF16)
            dk = dk + dot(grad, q * masks[e])
            dq = dq + dot(grad, k * masks[e], TN)
        dq_s[:, cols] = (dq * SCALE).astype(BF16)
        dk_s[:, cols] = (dk * SCALE).astype(BF16)

    @pl.when(pipe > 0)
    def _():
        branch = dot(dq_s[...], wq_v[...], NT)
        branch = branch + dot(dk_s[...], wk_v[...], NT)
        branch = branch + dot(vg_s[...], wv_v[...], NT)
        ret_tx[...] = branch.astype(BF16).reshape(nf, per, chans)

        def one(k, carry):
            to = lax.rem(me - k + nf, nf)
            pltpu.make_async_remote_copy(
                src_ref=ret_tx.at[k],
                dst_ref=ret_rx.at[me],
                send_sem=ret_sem.at[0],
                recv_sem=ret_sem.at[1],
                device_id={"frame": to, "pipe": pipe - 1},
                device_id_type=MESH,
            ).start()
            return carry

        lax.fori_loop(0, nf, one, 0)

    for j in range(2, messages):
        ring_step(j)

    for d in range(2):
        for j in range(max(0, messages - 2), messages):
            ring(d, j).wait_recv()
    for h in range(2):
        value = own(clip, h)
        for d in range(2):
            j = messages - 1 - (h + d) % 2
            if j >= 0:
                value = value + rs_rx[d, j].astype(F32)
        fin_f[h] = value
    for f in range(nf):
        at = slice(f * mine, (f + 1) * mine)
        fin_tx[f] = jnp.concatenate([fin_f[0, at, :], fin_f[1, at, :]], axis=0).astype(BF16)
    fin_rx[0] = fin_tx[me]
    spread(lambda to: fin_tx.at[to], fin_rx, fin_sem)

    @pl.when(pipe < np_ - 1)
    def _():
        wait_bytes(cot_rx, cot_sem.at[1])
        wait_bytes(ret_rx, ret_sem.at[1])
        sent[...] = (cot_rx[...].astype(F32) + ret_rx[...].astype(F32)).astype(BF16)

    @pl.when(pipe == np_ - 1)
    def _():
        sent[...] = jnp.zeros_like(sent)

    wait_bytes(fin_rx.at[others], fin_sem.at[1])
    total = jnp.sum(fin_rx[...].astype(F32), axis=0)
    for h in range(2):
        gvalue[:, h * half : (h + 1) * half] = total[h * mine : (h + 1) * mine]

    wait_bytes(acts_rx.at[others], acts_sem.at[0])
    wait_bytes(proj_rx.at[others], proj_sem.at[0])
    wait_bytes(fin_rx.at[others], fin_sem.at[0])
    for d in range(2):
        for j in range(messages):
            ring(d, j).wait_send()

    @pl.when(pipe > 0)
    def _():
        wait_bytes(cot_rx, cot_sem.at[0])
        wait_bytes(ret_rx, ret_sem.at[0])


def body(nf, ny, np_, acts, cotangent, w_query, w_key, w_value, w_out):
    per, places, chans = acts.shape[2:]
    inner = w_out.shape[2]
    rows = nf * per
    mine = inner // (nf * ny)
    messages = 2 * (ny // 2) - 1
    half = chans // 2
    by_place = [jnp.swapaxes(a[0, 0], 0, 1) for a in (acts, cotangent)]
    anywhere = pl.BlockSpec(memory_space=pl.ANY)
    in_vmem = pl.BlockSpec(memory_space=pltpu.VMEM)
    sent, gvalue = pl.pallas_call(
        functools.partial(kernel, nf, ny, np_),
        out_shape=(
            jax.ShapeDtypeStruct((places, per, chans), BF16),
            jax.ShapeDtypeStruct((mine, chans), F32),
        ),
        in_specs=[anywhere] * 6,
        out_specs=(in_vmem, in_vmem),
        scratch_shapes=[
            pltpu.VMEM((nf, per, chans), BF16),
            pltpu.VMEM((nf, per, inner), BF16),
            pltpu.VMEM((nf, per, inner), BF16),
            pltpu.VMEM((nf, per, chans), BF16),
            pltpu.VMEM((nf, per, chans), BF16),
            pltpu.VMEM((nf, per, chans), BF16),
            pltpu.VMEM((nf, per, chans), BF16),
            pltpu.VMEM((chans, inner), BF16),
            pltpu.VMEM((chans, inner), BF16),
            pltpu.VMEM((chans, inner), BF16),
            pltpu.VMEM((chans, inner), BF16),
            pltpu.VMEM((rows, inner), BF16),
            pltpu.VMEM((rows, inner), BF16),
            pltpu.VMEM((rows, inner), BF16),
            pltpu.VMEM((rows, inner), BF16),
            pltpu.VMEM((rows, inner), BF16),
            pltpu.VMEM((rows, inner), BF16),
            pltpu.VMEM((inner, inner), BF16),
            pltpu.VMEM((inner, rows), BF16),
            pltpu.VMEM((HEADS, rows, rows), F32),
            pltpu.VMEM((ny, mine * nf, chans), F32),
            pltpu.VMEM((2, messages, mine * nf, half), BF16),
            pltpu.VMEM((2, messages, mine * nf, half), BF16),
            pltpu.VMEM((2, mine * nf, half), F32),
            pltpu.VMEM((nf, 2 * mine, half), BF16),
            pltpu.VMEM((nf, 2 * mine, half), BF16),
            pltpu.SemaphoreType.DMA((6,)),
            pltpu.SemaphoreType.DMA((2,)),
            pltpu.SemaphoreType.DMA((2,)),
            pltpu.SemaphoreType.DMA((2,)),
            pltpu.SemaphoreType.DMA((2,)),
            pltpu.SemaphoreType.DMA((2,)),
            pltpu.SemaphoreType.DMA((2, messages)),
            pltpu.SemaphoreType.DMA((2, messages)),
        ],
        compiler_params=pltpu.CompilerParams(
            collective_id=0, has_side_effects=True, vmem_limit_bytes=56 * 1024 * 1024
        ),
        name="attention_backward",
    )(*by_place, w_query[0], w_key[0], w_value[0], w_out[0])
    return jnp.swapaxes(sent, 0, 1)[None, None], gvalue.T[None]


def solution(mesh):
    sizes = [mesh.shape[a] for a in ("frame", "dp", "pipe")]
    spread = P("pipe", "dp", "frame", None, None)
    return jax.shard_map(
        functools.partial(body, *sizes),
        mesh=mesh,
        in_specs=(spread, spread) + (P("pipe", None, None),) * 4,
        out_specs=(spread, P("pipe", None, ("frame", "dp"))),
        check_vma=False,
    )
```

time: 192 us -> 88 us (0.46)
  Pallas kernels: 0 us -> 81.4 us
  blocking collectives: 80.2 us -> 0 us
  waiting for transfers between devices: 50.4 us -> 0 us
  matrix products: 21.8 us -> 0 us
  between operations: 14.3 us -> 0.64 us
  starting transfers between devices: 8.73 us -> 0 us
  local copies, waits for them, and re-layouts: 12.2 us -> 5.51 us
  other arithmetic: 3.48 us -> 0 us
    pallas_call x0 -> x1, Pallas kernels: none -> 81.4 us  [body(): pl.pallas_call(functools.partial(kernel, nf, ny, np_), out_shape=(jax.Sha...]
    all_to_all x2 -> x0, blocking collectives: 80.2 us -> none  [the longest x1 48.1 us: in_one_piece(): lax.all_to_all(both, axis, split_axis=split_dim, concat_axis=concat_dim,...]
    reduce_scatter x2 -> x0, waiting for transfers between devices: 41.8 us -> none  [sum_by_axis(): nearer = lax.psum_scatter(shard, axes[0], scatter_dimension=dim, tiled=True)]
    dot_general x12 -> x0, matrix products: 19.4 us -> none  [the longest x3 7.05 us: project_heads(): jnp.dot(inputs, weight, preferred_element_type=jnp.float32)]
    all_to_all x1 -> x0, waiting for transfers between devices: 8.55 us -> none  [sum_at_owner(): parts = lax.all_to_all(in_blocks(shard, dim, count), axis, 0, 0, tiled=True)]
    all_to_all x1 -> x0, starting transfers between devices: 6.73 us -> none  [sum_at_owner(): parts = lax.all_to_all(in_blocks(shard, dim, count), axis, 0, 0, tiled=True)]
    convert_element_type x5 -> x0, local copies, waits for them, and re-layouts: 4.72 us -> none  [the longest x3 4.15 us: project_heads(): jnp.dot(inputs, weight, preferred_element_type=jnp.float32)]
    convert_element_type x4 -> x0, other arithmetic: 2.75 us -> none  [the longest x1 1.01 us: body(): frame_branch.astype(jnp.float32)]
  transfers between devices with their start and end apart: 4 -> 0, of which waited for: 3 -> 0; matrix products, arithmetic and copies ran while one was open for 6% -> 0% of each run, Pallas kernels for 0% -> 0%
where the time goes in v1:
time: 88 us; the launch traced here: 87.6 us
  Pallas kernels  81.4 us (93%)
  local copies, waits for them, and re-layouts  5.51 us (6%)
    pallas_call x1, Pallas kernels, body(): pl.pallas_call(functools.partial(kernel, nf, ny, np_), out_shape=(jax.Sha...  81.4 us
    unnamed x2, local copies, waits for them, and re-layouts  3.23 us
    transpose x1, local copies, waits for them, and re-layouts, body(): by_place = [jnp.swapaxes(a[0, 0], 0, 1) for a in (acts, cotangent)]  2.28 us

profile of v1, /device:TPU:6, one launch (start us, length us, event | category | flops | bytes accessed | tf_op | source)
XLA Modules:
  0.0 87.6 jit_solution(4814207667992339568)
XLA Ops:
  0.6 2.3 %copy_bitcast_fusion = (bf16[24,8,1280]{2,1,0:T(8,128)(2,1)}, bf16[24,8,1280]{2,1,0:T(8,128)(2,1)}) fusion(bf16[1,1,8,24,1280]{4,3,2,1,0:T(8,128)(2,1)} %param.7, bf16[1,1,8,24,1280]{4,3,2,1,0:T(8,128)(2,1)} %param.6), kind=kLoop, calls=%fused_computation | loop fusion | bytes 1966080 | tf_op jit(solution)/shard_map/transpose | solution.py:325
  2.9 81.4 %attention_backward.1 = (bf16[24,8,1280]{2,1,0:T(8,128)(2,1)}, f32[4,1280]{1,0:T(4,128)}) custom-call(bf16[24,8,1280]{2,1,0:T(8,128)(2,1)} %get-tuple-element.9.acts, bf16[24,8,1280]{2,1,0:T(8,128)(2,1)} %get-tuple-element.8.cot, bf16[1280,768]{1,0:T(8,128)(2,1)} %bitcast.18, bf16[1280,768]{1,0:T(8,128)(2,1)} %bitcast.19, bf16[1280,768]{1,0:T(8,128)(2,1)} %bitcast.20, ...), custom_call_target="tpu_custom_call" | custom-call | tf_op jit(solution)/shard_map/attention_backward/pallas_call | solution.py:328
  84.3 1.9 %copy.10 = bf16[1,1,8,24,1280]{4,3,2,1,0:T(8,128)(2,1)} copy(bf16[1,1,8,24,1280]{4,2,3,1,0:T(8,128)(2,1)} %bitcast.22) | data formatting | bytes 983040
  86.2 1.3 %copy.14 = f32[1,1280,4]{1,2,0:T(4,128)} copy(f32[1,1280,4]{1,2,0:T(4,128)} %bitcast.23) | data formatting | bytes 40960

commit v2 on v1

--- a/solution.py
+++ b/solution.py
@@ -45,6 +45,9 @@
     acts_rx,
     proj_rx,
     proj_tx,
+    acts_v,
+    acts_tx,
+    turn,
     cot_v,
     cot_rx,
     ret_tx,
@@ -76,6 +79,8 @@
     fin_sem,
     rs_send,
     rs_recv,
+    ready,
+    turn_over,
 ):
     me = lax.axis_index("frame")
     pipe = lax.axis_index("pipe")
@@ -93,9 +98,9 @@
     loads = []
     for i, (src, dst) in enumerate(
         (
+            (acts, acts_v),
+            (cot, cot_v),
             (w_out, wo_v),
-            (cot, cot_v),
-            (acts.at[me], acts_rx.at[0]),
             (w_query, wq_v),
             (w_key, wk_v),
             (w_value, wv_v),
@@ -108,57 +113,97 @@
     barrier = pltpu.get_barrier_semaphore()
     up = lax.rem(clip + 1, ny)
     down = lax.rem(clip + ny - 1, ny)
-
-    def greet(k, carry):
-        pl.semaphore_signal(
-            barrier, inc=1, device_id={"frame": lax.rem(me + k, nf)}, device_id_type=MESH
-        )
+    second = lax.rem(pipe, 2)
+    partner = pipe + 1 - 2 * second
+
+    def greet(b, carry):
+        pl.semaphore_signal(barrier, inc=1, device_id={"frame": b}, device_id_type=MESH)
         return carry
 
-    lax.fori_loop(1, nf, greet, 0)
+    lax.fori_loop(me + 1, nf, greet, 0)
     for y in (up, down):
         pl.semaphore_signal(barrier, inc=1, device_id={"dp": y}, device_id_type=MESH)
-    pl.semaphore_signal(
-        barrier, inc=1, device_id={"pipe": lax.rem(pipe + 1, np_)}, device_id_type=MESH
-    )
-    pl.semaphore_wait(barrier, nf + 2)
+    for p in (lax.rem(pipe + 1, np_), partner):
+        pl.semaphore_signal(barrier, inc=1, device_id={"pipe": p}, device_id_type=MESH)
+    pl.semaphore_wait(barrier, me + 4)
+
+    def answer(a, carry):
+        pl.semaphore_signal(ready.at[me], inc=1, device_id={"frame": a}, device_id_type=MESH)
+        return carry
+
+    lax.fori_loop(0, me, answer, 0)
 
     def shift_of(i):
         near = lax.div(i, 2)
         odd = lax.rem(i, 2)
         return (near + 1) * (1 - odd) + (nf - 1 - near) * odd
 
-    def spread(src_of, rx, sems):
-        def one(i, carry):
-            k = shift_of(i)
-            to = lax.rem(me + k, nf)
-            pltpu.make_async_remote_copy(
-                src_ref=src_of(to),
-                dst_ref=rx.at[k],
-                send_sem=sems.at[0],
-                recv_sem=sems.at[1],
-                device_id={"frame": to},
-                device_id_type=MESH,
-            ).start()
+    late = lax.div(2 * me, nf)
+
+    def send(tx, rx, sends, recvs, to):
+        pltpu.make_async_remote_copy(
+            src_ref=tx.at[to],
+            dst_ref=rx.at[me],
+            send_sem=sends,
+            recv_sem=recvs,
+            device_id={"frame": to},
+            device_id_type=MESH,
+        ).start()
+
+    def send_acts(to):
+        send(acts_tx, acts_rx, acts_sem.at[2], acts_sem.at[late], to)
+
+    def send_proj(to):
+        send(proj_tx, proj_rx, proj_sem.at[0], proj_sem.at[1], to)
+
+    def send_fin(to):
+        send(fin_tx, fin_rx, fin_sem.at[0], fin_sem.at[1], to)
+
+    def keep(tx, rx, sem):
+        pltpu.make_async_copy(tx.at[me], rx.at[me], sem).start()
+
+    def to_earlier(one):
+        def step(i, carry):
+            to = lax.rem(me + shift_of(i), nf)
+            pl.when(to < me)(lambda: one(to))
             return carry
 
-        lax.fori_loop(0, nf - 1, one, 0)
+        lax.fori_loop(0, nf - 1, step, 0)
 
     others = pl.ds(1, nf - 1)
 
-    spread(lambda to: acts.at[to], acts_rx, acts_sem)
-
+    at = lax.broadcasted_iota(jnp.int32, (rows, rows), 0)
+    column = lax.rem(at, per) * nf + lax.div(at, per)
+    turn[...] = jnp.where(
+        column == lax.broadcasted_iota(jnp.int32, (rows, rows), 1), 1.0, 0.0
+    ).astype(BF16)
     loads[0].wait()
+    acts_tx[...] = dot(turn[...], acts_v[...]).astype(BF16).reshape(nf, per, chans)
+    keep(acts_tx, acts_rx, acts_sem.at[late])
+
+    to_earlier(send_acts)
+
     loads[1].wait()
-    projected = dot(cot_v[...].reshape(rows, chans), wo_v[...]).astype(BF16)
-    proj_tx[...] = projected.reshape(nf, per, inner)
-    proj_rx[0] = proj_tx[me]
-    spread(lambda to: proj_tx.at[to], proj_rx, proj_sem)
+    loads[2].wait()
+    projected = dot(cot_v[...], wo_v[...]).astype(BF16)
+    proj_tx[...] = dot(turn[...], projected).astype(BF16).reshape(nf, per, inner)
+    keep(proj_tx, proj_rx, proj_sem.at[1])
+
+
+    to_earlier(send_proj)
+
+    def to_later(to, carry):
+        pl.semaphore_wait(ready.at[to], 1)
+        send_acts(to)
+        send_proj(to)
+        return carry
+
+    lax.fori_loop(me + 1, nf, to_later, 0)
 
     @pl.when(pipe > 0)
     def _():
         pltpu.make_async_remote_copy(
-            src_ref=cot,
+            src_ref=cot_v,
             dst_ref=cot_rx,
             send_sem=cot_sem.at[0],
             recv_sem=cot_sem.at[1],
@@ -172,14 +217,22 @@
         column == lax.broadcasted_iota(jnp.int32, (inner, inner), 1), 1.0, 0.0
     ).astype(BF16)
 
-    for load in loads[2:]:
+    wait_bytes(acts_rx.at[others], acts_sem.at[2])
+    wait_bytes(proj_rx.at[others], proj_sem.at[0])
+
+    for load in loads[3:]:
         load.wait()
-    wait_bytes(acts_rx.at[others], acts_sem.at[1])
+    few = nf // 2
+    for e in range(2):
+        slots = pl.ds(e * few, few)
+        block = pl.ds(e * few * per, few * per)
+        wait_bytes(acts_rx.at[slots], acts_sem.at[e])
+        inputs = acts_rx[slots].reshape(few * per, chans)
+        q_s[block, :] = dot(inputs, wq_v[...]).astype(BF16)
+        k_s[block, :] = dot(inputs, wk_v[...]).astype(BF16)
+        v_s[block, :] = dot(inputs, wv_v[...]).astype(BF16)
     inputs = acts_rx[...].reshape(rows, chans)
-    q_s[...] = dot(inputs, wq_v[...]).astype(BF16)
-    k_s[...] = dot(inputs, wk_v[...]).astype(BF16)
-    v_s[...] = dot(inputs, wv_v[...]).astype(BF16)
-    wait_bytes(proj_rx.at[others], proj_sem.at[1])
+    wait_bytes(proj_rx, proj_sem.at[1])
     lane = lax.broadcasted_iota(jnp.int32, (1, PAIR), 1)
     masks = [jnp.where(lane // HEAD_DIM == e, 1.0, 0.0).astype(BF16) for e in range(2)]
 
@@ -198,8 +251,11 @@
         vg_s[:, cols] = total.astype(BF16)
 
     vgt_b[...] = dot(order[...], vg_s[...], NT).astype(BF16)
-    for y in range(ny):
-        gv[y] = dot(vgt_b[y * size : (y + 1) * size, :], inputs)
+
+    def sum_for(away):
+        o = lax.rem(clip + away, ny)
+        at = pl.ds(pl.multiple_of(o * size, size), size)
+        gv[o] = dot(vgt_b[at, :], inputs)
 
     def own(o, h):
         return gv[o, :, h * half : (h + 1) * half]
@@ -226,8 +282,18 @@
             rs_tx[d, j] = value.astype(BF16)
             ring(d, j).start()
 
-    for j in range(min(2, messages)):
-        ring_step(j)
+    sum_for(reach)
+    ring_step(0)
+    if messages > 1:
+        sum_for(reach - 1)
+        sum_for(ny - reach + 1)
+        ring_step(1)
+    for away in range(reach - 1):
+        sum_for(away)
+        if away:
+            sum_for(ny - away)
+    if messages == 1:
+        sum_for(0)
 
     for pair in range(PAIRS):
         cols = pl.ds(pair * PAIR, PAIR)
@@ -247,6 +313,9 @@
         dq_s[:, cols] = (dq * SCALE).astype(BF16)
         dk_s[:, cols] = (dk * SCALE).astype(BF16)
 
+    if messages > 2:
+        ring_step(2)
+
     @pl.when(pipe > 0)
     def _():
         branch = dot(dq_s[...], wq_v[...], NT)
@@ -254,10 +323,10 @@
         branch = branch + dot(vg_s[...], wv_v[...], NT)
         ret_tx[...] = branch.astype(BF16).reshape(nf, per, chans)
 
-        def one(k, carry):
-            to = lax.rem(me - k + nf, nf)
+        def one(i, carry):
+            to = lax.rem(me + shift_of(i) * jnp.minimum(nf - 1 - i, 1), nf)
             pltpu.make_async_remote_copy(
-                src_ref=ret_tx.at[k],
+                src_ref=ret_tx.at[to],
                 dst_ref=ret_rx.at[me],
                 send_sem=ret_sem.at[0],
                 recv_sem=ret_sem.at[1],
@@ -268,7 +337,7 @@
 
         lax.fori_loop(0, nf, one, 0)
 
-    for j in range(2, messages):
+    for j in range(3, messages):
         ring_step(j)
 
     for d in range(2):
@@ -284,26 +353,30 @@
     for f in range(nf):
         at = slice(f * mine, (f + 1) * mine)
         fin_tx[f] = jnp.concatenate([fin_f[0, at, :], fin_f[1, at, :]], axis=0).astype(BF16)
-    fin_rx[0] = fin_tx[me]
-    spread(lambda to: fin_tx.at[to], fin_rx, fin_sem)
+    keep(fin_tx, fin_rx, fin_sem.at[1])
+
+    def finish(i, carry):
+        send_fin(lax.rem(me + shift_of(i), nf))
+        return carry
+
+    lax.fori_loop(0, nf - 1, finish, 0)
 
     @pl.when(pipe < np_ - 1)
     def _():
         wait_bytes(cot_rx, cot_sem.at[1])
         wait_bytes(ret_rx, ret_sem.at[1])
-        sent[...] = (cot_rx[...].astype(F32) + ret_rx[...].astype(F32)).astype(BF16)
+        branch = dot(turn[...], ret_rx[...].reshape(rows, chans), TN)
+        sent[...] = (cot_rx[...].astype(F32) + branch).astype(BF16)
 
     @pl.when(pipe == np_ - 1)
     def _():
         sent[...] = jnp.zeros_like(sent)
 
-    wait_bytes(fin_rx.at[others], fin_sem.at[1])
+    wait_bytes(fin_rx, fin_sem.at[1])
     total = jnp.sum(fin_rx[...].astype(F32), axis=0)
     for h in range(2):
         gvalue[:, h * half : (h + 1) * half] = total[h * mine : (h + 1) * mine]
 
-    wait_bytes(acts_rx.at[others], acts_sem.at[0])
-    wait_bytes(proj_rx.at[others], proj_sem.at[0])
     wait_bytes(fin_rx.at[others], fin_sem.at[0])
     for d in range(2):
         for j in range(messages):
@@ -322,13 +395,13 @@
     mine = inner // (nf * ny)
     messages = 2 * (ny // 2) - 1
     half = chans // 2
-    by_place = [jnp.swapaxes(a[0, 0], 0, 1) for a in (acts, cotangent)]
+    flat = [a[0, 0].reshape(per * places, chans) for a in (acts, cotangent)]
     anywhere = pl.BlockSpec(memory_space=pl.ANY)
     in_vmem = pl.BlockSpec(memory_space=pltpu.VMEM)
     sent, gvalue = pl.pallas_call(
         functools.partial(kernel, nf, ny, np_),
         out_shape=(
-            jax.ShapeDtypeStruct((places, per, chans), BF16),
+            jax.ShapeDtypeStruct((rows, chans), BF16),
             jax.ShapeDtypeStruct((mine, chans), F32),
         ),
         in_specs=[anywhere] * 6,
@@ -337,8 +410,11 @@
             pltpu.VMEM((nf, per, chans), BF16),
             pltpu.VMEM((nf, per, inner), BF16),
             pltpu.VMEM((nf, per, inner), BF16),
+            pltpu.VMEM((rows, chans), BF16),
             pltpu.VMEM((nf, per, chans), BF16),
-            pltpu.VMEM((nf, per, chans), BF16),
+            pltpu.VMEM((rows, rows), BF16),
+            pltpu.VMEM((rows, chans), BF16),
+            pltpu.VMEM((rows, chans), BF16),
             pltpu.VMEM((nf, per, chans), BF16),
             pltpu.VMEM((nf, per, chans), BF16),
             pltpu.VMEM((chans, inner), BF16),
@@ -361,20 +437,22 @@
             pltpu.VMEM((nf, 2 * mine, half), BF16),
             pltpu.VMEM((nf, 2 * mine, half), BF16),
             pltpu.SemaphoreType.DMA((6,)),
-            pltpu.SemaphoreType.DMA((2,)),
+            pltpu.SemaphoreType.DMA((3,)),
             pltpu.SemaphoreType.DMA((2,)),
             pltpu.SemaphoreType.DMA((2,)),
             pltpu.SemaphoreType.DMA((2,)),
             pltpu.SemaphoreType.DMA((2,)),
             pltpu.SemaphoreType.DMA((2, messages)),
             pltpu.SemaphoreType.DMA((2, messages)),
+            pltpu.SemaphoreType.REGULAR((nf,)),
+            pltpu.SemaphoreType.REGULAR,
         ],
         compiler_params=pltpu.CompilerParams(
             collective_id=0, has_side_effects=True, vmem_limit_bytes=56 * 1024 * 1024
         ),
         name="attention_backward",
-    )(*by_place, w_query[0], w_key[0], w_value[0], w_out[0])
-    return jnp.swapaxes(sent, 0, 1)[None, None], gvalue.T[None]
+    )(*flat, w_query[0], w_key[0], w_value[0], w_out[0])
+    return sent.reshape(1, 1, per, places, chans), gvalue.T[None]
 
 
 def solution(mesh):

time: 88 us -> 84.7 us (0.963)
  local copies, waits for them, and re-layouts: 5.51 us -> 3.17 us
    transpose x1 -> x0, local copies, waits for them, and re-layouts: 2.28 us -> none  [body(): by_place = [jnp.swapaxes(a[0, 0], 0, 1) for a in (acts, cotangent)]]
where the time goes in v2:
time: 84.7 us; the launch traced here: 84.5 us
  Pallas kernels  80.7 us (95%)
  local copies, waits for them, and re-layouts  3.17 us (4%)
    pallas_call x1, Pallas kernels, body(): pl.pallas_call(functools.partial(kernel, nf, ny, np_), out_shape=(jax.Sha...  80.7 us
    unnamed x2, local copies, waits for them, and re-layouts  3.17 us

profile of v2, /device:TPU:6, one launch (start us, length us, event | category | flops | bytes accessed | tf_op | source)
XLA Modules:
  0.0 84.5 jit_solution(7584082719551150718)
XLA Ops:
  0.6 80.7 %attention_backward.1 = (bf16[192,1280]{1,0:T(8,128)(2,1)}, f32[4,1280]{1,0:T(4,128)}) custom-call(bf16[192,1280]{1,0:T(8,128)(2,1)} %bitcast.14, bf16[192,1280]{1,0:T(8,128)(2,1)} %bitcast.15, bf16[1280,768]{1,0:T(8,128)(2,1)} %bitcast.10, bf16[1280,768]{1,0:T(8,128)(2,1)} %bitcast.11, bf16[1280,768]{1,0:T(8,128)(2,1)} %bitcast.12, bf16[1280,768]{1,0:T(8,128)(2,1)} %bitcast.13), custom_call_target="tpu_custom_call" | custom-call | tf_op jit(solution)/shard_map/attention_backward/pallas_call | solution.py:401
  81.3 1.8 %copy.10 = bf16[1,1,8,24,1280]{4,3,2,1,0:T(8,128)(2,1)} copy(bf16[1,1,8,24,1280]{4,3,2,1,0:T(8,128)(2,1)} %bitcast.16) | data formatting | bytes 983040
  83.2 1.3 %copy.11 = f32[1,1280,4]{1,2,0:T(4,128)} copy(f32[1,1280,4]{1,2,0:T(4,128)} %bitcast.17) | data formatting | bytes 40960

commit v3 on v2

--- a/solution.py
+++ b/solution.py
@@ -66,6 +66,8 @@
     vgt_b,
     prob,
     gv,
+    px_tx,
+    px_rx,
     rs_tx,
     rs_rx,
     fin_f,
@@ -79,8 +81,9 @@
     fin_sem,
     rs_send,
     rs_recv,
+    px_send,
+    px_recv,
     ready,
-    turn_over,
 ):
     me = lax.axis_index("frame")
     pipe = lax.axis_index("pipe")
@@ -91,9 +94,11 @@
     rows = nf * per
     half = chans // 2
     reach = ny // 2
-    messages = 2 * reach - 1
     mine = gvalue.shape[0]
     size = mine * nf
+    part = size // 2
+    side = lax.rem(me, 2)
+    beside = me + 1 - 2 * side
 
     loads = []
     for i, (src, dst) in enumerate(
@@ -113,8 +118,6 @@
     barrier = pltpu.get_barrier_semaphore()
     up = lax.rem(clip + 1, ny)
     down = lax.rem(clip + ny - 1, ny)
-    second = lax.rem(pipe, 2)
-    partner = pipe + 1 - 2 * second
 
     def greet(b, carry):
         pl.semaphore_signal(barrier, inc=1, device_id={"frame": b}, device_id_type=MESH)
@@ -123,9 +126,10 @@
     lax.fori_loop(me + 1, nf, greet, 0)
     for y in (up, down):
         pl.semaphore_signal(barrier, inc=1, device_id={"dp": y}, device_id_type=MESH)
-    for p in (lax.rem(pipe + 1, np_), partner):
-        pl.semaphore_signal(barrier, inc=1, device_id={"pipe": p}, device_id_type=MESH)
-    pl.semaphore_wait(barrier, me + 4)
+    pl.semaphore_signal(
+        barrier, inc=1, device_id={"pipe": lax.rem(pipe + 1, np_)}, device_id_type=MESH
+    )
+    pl.semaphore_wait(barrier, me + 3)
 
     def answer(a, carry):
         pl.semaphore_signal(ready.at[me], inc=1, device_id={"frame": a}, device_id_type=MESH)
@@ -188,8 +192,6 @@
     projected = dot(cot_v[...], wo_v[...]).astype(BF16)
     proj_tx[...] = dot(turn[...], projected).astype(BF16).reshape(nf, per, inner)
     keep(proj_tx, proj_rx, proj_sem.at[1])
-
-
     to_earlier(send_proj)
 
     def to_later(to, carry):
@@ -212,7 +214,9 @@
         ).start()
 
     at = lax.broadcasted_iota(jnp.int32, (inner, inner), 0)
-    column = lax.rem(lax.div(at, mine), nf) * (ny * mine) + lax.div(at, size) * mine + lax.rem(at, mine)
+    group = lax.rem(lax.div(at, mine), nf)
+    frame = 2 * lax.rem(group, nf // 2) + lax.div(group, nf // 2)
+    column = frame * (ny * mine) + lax.div(at, size) * mine + lax.rem(at, mine)
     order[...] = jnp.where(
         column == lax.broadcasted_iota(jnp.int32, (inner, inner), 1), 1.0, 0.0
     ).astype(BF16)
@@ -257,43 +261,82 @@
         at = pl.ds(pl.multiple_of(o * size, size), size)
         gv[o] = dot(vgt_b[at, :], inputs)
 
-    def own(o, h):
-        return gv[o, :, h * half : (h + 1) * half]
-
-    def ring(d, j):
+    def beside_copy(t):
         return pltpu.make_async_remote_copy(
-            src_ref=rs_tx.at[d, j],
-            dst_ref=rs_rx.at[d, j],
-            send_sem=rs_send.at[d, j],
-            recv_sem=rs_recv.at[d, j],
+            src_ref=px_tx.at[t],
+            dst_ref=px_rx.at[t],
+            send_sem=px_send.at[t],
+            recv_sem=px_recv.at[t],
+            device_id={"frame": beside},
+            device_id_type=MESH,
+        )
+
+    def turn_of(d, away):
+        if away == 0:
+            return ny - 1
+        return 0 if away == reach else 2 * (reach - away) - 1 + d
+
+    def swap_sides(d, away):
+        t = turn_of(d, away)
+        away = away if d == 0 else ny - away
+        sum_for(away)
+        o = lax.rem(clip + away, ny)
+        at = pl.ds(pl.multiple_of((1 - side) * part, part), part)
+        px_tx[t] = gv[o, at, :half].astype(BF16)
+        beside_copy(t).start()
+
+    def own(d, q, away):
+        o = lax.rem(clip + (away if d == 0 else ny - away), ny)
+        if q == 0:
+            t = turn_of(d, away)
+            beside_copy(t).wait_recv()
+            at = pl.ds(pl.multiple_of(side * part, part), part)
+            return gv[o, at, :half] + px_rx[t].astype(F32)
+        return gv[o, (q - 1) * part : q * part, half:]
+
+    far = ((reach, reach, reach - 1), (reach - 1, reach - 1, reach))
+
+    def ring(d, q, away):
+        return pltpu.make_async_remote_copy(
+            src_ref=rs_tx.at[d, q, away - 1],
+            dst_ref=rs_rx.at[d, q, away - 1],
+            send_sem=rs_send.at[d, q, away - 1],
+            recv_sem=rs_recv.at[d, q, away - 1],
             device_id={"dp": (up, down)[d]},
             device_id_type=MESH,
         )
 
-    def ring_step(j):
-        away = reach - (j + 1) // 2
-        for d in range(2):
-            h = (j + d) % 2
-            o = lax.rem(clip + (away if d == 0 else ny - away), ny)
-            value = own(o, h)
-            if j >= 2:
-                ring(d, j - 2).wait_recv()
-                value = value + rs_rx[d, j - 2].astype(F32)
-            rs_tx[d, j] = value.astype(BF16)
-            ring(d, j).start()
-
-    sum_for(reach)
-    ring_step(0)
-    if messages > 1:
-        sum_for(reach - 1)
-        sum_for(ny - reach + 1)
-        ring_step(1)
-    for away in range(reach - 1):
-        sum_for(away)
-        if away:
-            sum_for(ny - away)
-    if messages == 1:
-        sum_for(0)
+    def pass_on(d, q, away):
+        value = own(d, q, away)
+        if away < far[d][q]:
+            ring(d, q, away + 1).wait_recv()
+            value = value + rs_rx[d, q, away].astype(F32)
+        rs_tx[d, q, away - 1] = value.astype(BF16)
+        ring(d, q, away).start()
+
+    def long_ways(away):
+        for d, q in ((1, 2), (0, 1), (0, 0)):
+            pass_on(d, q, away)
+
+    def short_ways(away):
+        for d, q in ((0, 2), (1, 1), (1, 0)):
+            pass_on(d, q, away)
+
+    swap_sides(0, reach)
+    pass_on(1, 2, reach)
+    pass_on(0, 1, reach)
+    if reach > 1:
+        swap_sides(0, reach - 1)
+        swap_sides(1, reach - 1)
+        pass_on(0, 2, reach - 1)
+        pass_on(1, 1, reach - 1)
+    for away in range(reach - 2, 0, -1):
+        swap_sides(0, away)
+        swap_sides(1, away)
+    swap_sides(0, 0)
+    pass_on(0, 0, reach)
+    if reach > 1:
+        pass_on(1, 0, reach - 1)
 
     for pair in range(PAIRS):
         cols = pl.ds(pair * PAIR, PAIR)
@@ -313,9 +356,6 @@
         dq_s[:, cols] = (dq * SCALE).astype(BF16)
         dk_s[:, cols] = (dk * SCALE).astype(BF16)
 
-    if messages > 2:
-        ring_step(2)
-
     @pl.when(pipe > 0)
     def _():
         branch = dot(dq_s[...], wq_v[...], NT)
@@ -337,22 +377,23 @@
 
         lax.fori_loop(0, nf, one, 0)
 
-    for j in range(3, messages):
-        ring_step(j)
-
-    for d in range(2):
-        for j in range(max(0, messages - 2), messages):
-            ring(d, j).wait_recv()
-    for h in range(2):
-        value = own(clip, h)
+    for away in range(reach - 1, 0, -1):
+        long_ways(away)
+        if away > 1:
+            short_ways(away - 1)
+
+    for q in (1, 2, 0):
+        value = own(0, q, 0)
         for d in range(2):
-            j = messages - 1 - (h + d) % 2
-            if j >= 0:
-                value = value + rs_rx[d, j].astype(F32)
-        fin_f[h] = value
+            if far[d][q] > 0:
+                ring(d, q, 1).wait_recv()
+                value = value + rs_rx[d, q, 0].astype(F32)
+        fin_f[q] = value
+    zero = jnp.zeros((mine, half), F32)
     for f in range(nf):
-        at = slice(f * mine, (f + 1) * mine)
-        fin_tx[f] = jnp.concatenate([fin_f[0, at, :], fin_f[1, at, :]], axis=0).astype(BF16)
+        at = slice((f // 2) * mine, (f // 2 + 1) * mine)
+        first = jnp.where(side == f % 2, fin_f[0, at, :], zero)
+        fin_tx[f] = jnp.concatenate([first, fin_f[1 + f % 2, at, :]], axis=0).astype(BF16)
     keep(fin_tx, fin_rx, fin_sem.at[1])
 
     def finish(i, carry):
@@ -378,9 +419,12 @@
         gvalue[:, h * half : (h + 1) * half] = total[h * mine : (h + 1) * mine]
 
     wait_bytes(fin_rx.at[others], fin_sem.at[0])
+    for t in range(ny):
+        beside_copy(t).wait_send()
     for d in range(2):
-        for j in range(messages):
-            ring(d, j).wait_send()
+        for q in range(3):
+            for away in range(far[d][q], 0, -1):
+                ring(d, q, away).wait_send()
 
     @pl.when(pipe > 0)
     def _():
@@ -393,7 +437,7 @@
     inner = w_out.shape[2]
     rows = nf * per
     mine = inner // (nf * ny)
-    messages = 2 * (ny // 2) - 1
+    reach = ny // 2
     half = chans // 2
     flat = [a[0, 0].reshape(per * places, chans) for a in (acts, cotangent)]
     anywhere = pl.BlockSpec(memory_space=pl.ANY)
@@ -431,9 +475,11 @@
             pltpu.VMEM((inner, rows), BF16),
             pltpu.VMEM((HEADS, rows, rows), F32),
             pltpu.VMEM((ny, mine * nf, chans), F32),
-            pltpu.VMEM((2, messages, mine * nf, half), BF16),
-            pltpu.VMEM((2, messages, mine * nf, half), BF16),
-            pltpu.VMEM((2, mine * nf, half), F32),
+            pltpu.VMEM((ny, mine * nf // 2, half), BF16),
+            pltpu.VMEM((ny, mine * nf // 2, half), BF16),
+            pltpu.VMEM((2, 3, reach, mine * nf // 2, half), BF16),
+            pltpu.VMEM((2, 3, reach, mine * nf // 2, half), BF16),
+            pltpu.VMEM((3, mine * nf // 2, half), F32),
             pltpu.VMEM((nf, 2 * mine, half), BF16),
             pltpu.VMEM((nf, 2 * mine, half), BF16),
             pltpu.SemaphoreType.DMA((6,)),
@@ -442,13 +488,14 @@
             pltpu.SemaphoreType.DMA((2,)),
             pltpu.SemaphoreType.DMA((2,)),
             pltpu.SemaphoreType.DMA((2,)),
-            pltpu.SemaphoreType.DMA((2, messages)),
-            pltpu.SemaphoreType.DMA((2, messages)),
+            pltpu.SemaphoreType.DMA((2, 3, reach)),
+            pltpu.SemaphoreType.DMA((2, 3, reach)),
+            pltpu.SemaphoreType.DMA((ny,)),
+            pltpu.SemaphoreType.DMA((ny,)),
             pltpu.SemaphoreType.REGULAR((nf,)),
-            pltpu.SemaphoreType.REGULAR,
         ],
         compiler_params=pltpu.CompilerParams(
-            collective_id=0, has_side_effects=True, vmem_limit_bytes=56 * 1024 * 1024
+            collective_id=0, has_side_effects=True, vmem_limit_bytes=53 * 1024 * 1024
         ),
         name="attention_backward",
     )(*flat, w_query[0], w_key[0], w_value[0], w_out[0])

time: 84.7 us -> 85.3 us (level)
  Pallas kernels: 80.7 us -> 83.1 us
  local copies, waits for them, and re-layouts: 3.17 us -> 1.39 us
    pallas_call x1, Pallas kernels: 80.7 us -> 83.1 us  [body(): pl.pallas_call(functools.partial(kernel, nf, ny, np_), out_shape=(jax.Sha...]
    unnamed x2, local copies, waits for them, and re-layouts: 3.17 us -> 1.39 us
where the time goes in v3:
time: 85.3 us; the launch traced here: 85.1 us
  Pallas kernels  83.1 us (97%)
  local copies, waits for them, and re-layouts  1.39 us (2%)
    pallas_call x1, Pallas kernels, body(): pl.pallas_call(functools.partial(kernel, nf, ny, np_), out_shape=(jax.Sha...  83.1 us

profile of v3, /device:TPU:6, one launch (start us, length us, event | category | flops | bytes accessed | tf_op | source)
XLA Modules:
  0.0 85.1 jit_solution(17993350418024069947)
XLA Ops:
  0.6 83.1 %attention_backward.1 = (bf16[192,1280]{1,0:T(8,128)(2,1)S(1)}, f32[4,1280]{1,0:T(4,128)S(1)}) custom-call(bf16[192,1280]{1,0:T(8,128)(2,1)} %bitcast.16, bf16[192,1280]{1,0:T(8,128)(2,1)} %bitcast.17, bf16[1280,768]{1,0:T(8,128)(2,1)} %bitcast.12, bf16[1280,768]{1,0:T(8,128)(2,1)} %bitcast.13, bf16[1280,768]{1,0:T(8,128)(2,1)} %bitcast.14, ...), custom_call_target="tpu_custom_call" | custom-call | tf_op jit(solution)/shard_map/attention_backward/pallas_call | solution.py:445
  83.8 0.8 copy.10
  84.5 0.6 copy.11

commit v4 on v2

--- a/solution.py
+++ b/solution.py
@@ -80,7 +80,6 @@
     rs_send,
     rs_recv,
     ready,
-    turn_over,
 ):
     me = lax.axis_index("frame")
     pipe = lax.axis_index("pipe")
@@ -113,8 +112,6 @@
     barrier = pltpu.get_barrier_semaphore()
     up = lax.rem(clip + 1, ny)
     down = lax.rem(clip + ny - 1, ny)
-    second = lax.rem(pipe, 2)
-    partner = pipe + 1 - 2 * second
 
     def greet(b, carry):
         pl.semaphore_signal(barrier, inc=1, device_id={"frame": b}, device_id_type=MESH)
@@ -123,9 +120,10 @@
     lax.fori_loop(me + 1, nf, greet, 0)
     for y in (up, down):
         pl.semaphore_signal(barrier, inc=1, device_id={"dp": y}, device_id_type=MESH)
-    for p in (lax.rem(pipe + 1, np_), partner):
-        pl.semaphore_signal(barrier, inc=1, device_id={"pipe": p}, device_id_type=MESH)
-    pl.semaphore_wait(barrier, me + 4)
+    pl.semaphore_signal(
+        barrier, inc=1, device_id={"pipe": lax.rem(pipe + 1, np_)}, device_id_type=MESH
+    )
+    pl.semaphore_wait(barrier, me + 3)
 
     def answer(a, carry):
         pl.semaphore_signal(ready.at[me], inc=1, device_id={"frame": a}, device_id_type=MESH)
@@ -164,7 +162,7 @@
 
     def to_earlier(one):
         def step(i, carry):
-            to = lax.rem(me + shift_of(i), nf)
+            to = lax.rem(me + shift_of(nf - 2 - i), nf)
             pl.when(to < me)(lambda: one(to))
             return carry
 
@@ -188,8 +186,6 @@
     projected = dot(cot_v[...], wo_v[...]).astype(BF16)
     proj_tx[...] = dot(turn[...], projected).astype(BF16).reshape(nf, per, inner)
     keep(proj_tx, proj_rx, proj_sem.at[1])
-
-
     to_earlier(send_proj)
 
     def to_later(to, carry):
@@ -230,7 +226,6 @@
         inputs = acts_rx[slots].reshape(few * per, chans)
         q_s[block, :] = dot(inputs, wq_v[...]).astype(BF16)
         k_s[block, :] = dot(inputs, wk_v[...]).astype(BF16)
-        v_s[block, :] = dot(inputs, wv_v[...]).astype(BF16)
     inputs = acts_rx[...].reshape(rows, chans)
     wait_bytes(proj_rx, proj_sem.at[1])
     lane = lax.broadcasted_iota(jnp.int32, (1, PAIR), 1)
@@ -295,6 +290,7 @@
     if messages == 1:
         sum_for(0)
 
+    v_s[...] = dot(inputs, wv_v[...]).astype(BF16)
     for pair in range(PAIRS):
         cols = pl.ds(pair * PAIR, PAIR)
         q = q_s[:, cols]
@@ -313,9 +309,6 @@
         dq_s[:, cols] = (dq * SCALE).astype(BF16)
         dk_s[:, cols] = (dk * SCALE).astype(BF16)
 
-    if messages > 2:
-        ring_step(2)
-
     @pl.when(pipe > 0)
     def _():
         branch = dot(dq_s[...], wq_v[...], NT)
@@ -337,7 +330,7 @@
 
         lax.fori_loop(0, nf, one, 0)
 
-    for j in range(3, messages):
+    for j in range(2, messages):
         ring_step(j)
 
     for d in range(2):
@@ -445,10 +438,9 @@
             pltpu.SemaphoreType.DMA((2, messages)),
             pltpu.SemaphoreType.DMA((2, messages)),
             pltpu.SemaphoreType.REGULAR((nf,)),
-            pltpu.SemaphoreType.REGULAR,
         ],
         compiler_params=pltpu.CompilerParams(
-            collective_id=0, has_side_effects=True, vmem_limit_bytes=56 * 1024 * 1024
+            collective_id=0, has_side_effects=True, vmem_limit_bytes=53 * 1024 * 1024
         ),
         name="attention_backward",
     )(*flat, w_query[0], w_key[0], w_value[0], w_out[0])

time: 84.7 us -> 80.9 us (0.955)
  Pallas kernels: 80.7 us -> 78.6 us
  local copies, waits for them, and re-layouts: 3.17 us -> 1.39 us
    pallas_call x1, Pallas kernels: 80.7 us -> 78.6 us  [body(): pl.pallas_call(functools.partial(kernel, nf, ny, np_), out_shape=(jax.Sha...]
    unnamed x2, local copies, waits for them, and re-layouts: 3.17 us -> 1.39 us
where the time goes in v4:
time: 80.9 us; the launch traced here: 80.6 us
  Pallas kernels  78.6 us (97%)
  local copies, waits for them, and re-layouts  1.39 us (2%)
    pallas_call x1, Pallas kernels, body(): pl.pallas_call(functools.partial(kernel, nf, ny, np_), out_shape=(jax.Sha...  78.6 us

profile of v4, /device:TPU:6, one launch (start us, length us, event | category | flops | bytes accessed | tf_op | source)
XLA Modules:
  0.0 80.6 jit_solution(7112680276475847844)
XLA Ops:
  0.6 78.6 %attention_backward.1 = (bf16[192,1280]{1,0:T(8,128)(2,1)S(1)}, f32[4,1280]{1,0:T(4,128)S(1)}) custom-call(bf16[192,1280]{1,0:T(8,128)(2,1)} %bitcast.16, bf16[192,1280]{1,0:T(8,128)(2,1)} %bitcast.17, bf16[1280,768]{1,0:T(8,128)(2,1)} %bitcast.12, bf16[1280,768]{1,0:T(8,128)(2,1)} %bitcast.13, bf16[1280,768]{1,0:T(8,128)(2,1)} %bitcast.14, ...), custom_call_target="tpu_custom_call" | custom-call | tf_op jit(solution)/shard_map/attention_backward/pallas_call | solution.py:394
  79.2 0.8 copy.10
  80.0 0.6 copy.11

commit v5 on v4

--- a/solution.py
+++ b/solution.py
@@ -316,22 +316,30 @@
         branch = branch + dot(vg_s[...], wv_v[...], NT)
         ret_tx[...] = branch.astype(BF16).reshape(nf, per, chans)
 
-        def one(i, carry):
-            to = lax.rem(me + shift_of(i) * jnp.minimum(nf - 1 - i, 1), nf)
-            pltpu.make_async_remote_copy(
-                src_ref=ret_tx.at[to],
-                dst_ref=ret_rx.at[me],
-                send_sem=ret_sem.at[0],
-                recv_sem=ret_sem.at[1],
-                device_id={"frame": to, "pipe": pipe - 1},
-                device_id_type=MESH,
-            ).start()
-            return carry
-
-        lax.fori_loop(0, nf, one, 0)
-
-    for j in range(2, messages):
-        ring_step(j)
+    def give_back(i, carry):
+        to = lax.rem(me + shift_of(i) * jnp.minimum(nf - 1 - i, 1), nf)
+        pltpu.make_async_remote_copy(
+            src_ref=ret_tx.at[to],
+            dst_ref=ret_rx.at[me],
+            send_sem=ret_sem.at[0],
+            recv_sem=ret_sem.at[1],
+            device_id={"frame": to, "pipe": pipe - 1},
+            device_id_type=MESH,
+        ).start()
+        return carry
+
+    def give_back_some(first, last):
+        @pl.when(pipe > 0)
+        def _():
+            lax.fori_loop(first, last, give_back, 0)
+
+    few = -(-nf // 3)
+    give_back_some(0, few)
+    for j in range(2, max(messages, 3 + 1)):
+        if j < messages:
+            ring_step(j)
+        if j <= 3:
+            give_back_some((j - 1) * few, min((j) * few, nf))
 
     for d in range(2):
         for j in range(max(0, messages - 2), messages):

time: 80.9 us -> 81 us (level)
  no operation moved by 1% of the time
where the time goes in v5:
time: 81 us; the launch traced here: 80.6 us
  Pallas kernels  78.6 us (97%)
  local copies, waits for them, and re-layouts  1.39 us (2%)
    pallas_call x1, Pallas kernels, body(): pl.pallas_call(functools.partial(kernel, nf, ny, np_), out_shape=(jax.Sha...  78.6 us

profile of v5, /device:TPU:6, one launch (start us, length us, event | category | flops | bytes accessed | tf_op | source)
XLA Modules:
  0.0 80.6 jit_solution(8669580815311699533)
XLA Ops:
  0.6 78.6 %attention_backward.1 = (bf16[192,1280]{1,0:T(8,128)(2,1)S(1)}, f32[4,1280]{1,0:T(4,128)S(1)}) custom-call(bf16[192,1280]{1,0:T(8,128)(2,1)} %bitcast.16, bf16[192,1280]{1,0:T(8,128)(2,1)} %bitcast.17, bf16[1280,768]{1,0:T(8,128)(2,1)} %bitcast.12, bf16[1280,768]{1,0:T(8,128)(2,1)} %bitcast.13, bf16[1280,768]{1,0:T(8,128)(2,1)} %bitcast.14, ...), custom_call_target="tpu_custom_call" | custom-call | tf_op jit(solution)/shard_map/attention_backward/pallas_call | solution.py:402
  79.2 0.8 copy.10
  80.0 0.6 copy.11
